TPU v7x, 32 devices: a whole 2x2x4 slice. The times are simulated.
32 devices in a mesh: dp: 8 (over z, y), fsdp: 4 (over x, core).
Axes of the slice: x: 2, y: 2, z: 4, core: 2. Of those that a mesh axis runs over, the one named last changes fastest.
Arguments:
- features: bfloat16 [32, 8, 256, 128], P(('dp', 'fsdp')), may hold values from -60 to 60, as said below
- pick_index: int32 [32, 8, 2], P(('dp', 'fsdp')), may hold values from 0 to 255
- good_channel: int32 [32, 8], P(('dp', 'fsdp')), may hold values 0 or 1
- conv_weight: bfloat16 [1152, 128], P(None, 'fsdp'), may hold values from -0.1875 to 0.1875
- conv_bias: bfloat16 [1, 128], P(None, 'fsdp'), may hold values from -3 to 3
- head_weight: bfloat16 [2, 128], P(None, 'fsdp'), may hold values from -0.5 to 0.5
- head_bias: float32 [2], replicated, may hold values from -2 to 2
Outputs:
- grad_conv_weight: float32 [1152, 128], P('dp', 'fsdp')
- grad_conv_bias: float32 [1, 128], P(None, 'fsdp')
- grad_head_weight: float32 [2, 128], P(None, 'fsdp')
- grad_head_bias: float32 [2], replicated
- grad_features: bfloat16 [32, 8, 256, 128], P(('dp', 'fsdp'))
Inputs may be any that keep to these rules, and one draw needn't show every extreme that they name: `features`: real-valued feature maps.
All inputs are finite; a program needn't handle non-finite values. No bound on the sum of `good_channel` on one device may be relied on, other than what follows from the above.
Results may differ from a plain program's by a relative error of at most 0.007.
Values may be sent and summed in bfloat16 or wider, within the bound.
A program may use at most 64 MiB of HBM per device.

v0:
```python
import jax
import jax.numpy as jnp
from jax import lax
from jax.sharding import PartitionSpec as P

SIGMA = 20


def local_grads(features, pick_index, good_channel, conv_weight, conv_bias, head_weight, head_bias):
    patch_count, row_count, sample_count, width = features.shape
    cells = patch_count * row_count * sample_count
    padded = jnp.pad(features, ((0, 0), (1, 1), (1, 1), (0, 0)))
    preact = jnp.zeros((cells, width), jnp.float32) + conv_bias.astype(jnp.float32)
    shifted = []
    for tap_index in range(9):
        offset_row = tap_index // 3
        offset_col = tap_index % 3
        window = padded[
            :, offset_row : offset_row + row_count, offset_col : offset_col + sample_count, :
        ].reshape(cells, width)
        shifted.append(window)
        preact = preact + jnp.dot(
            window,
            conv_weight[tap_index * width : (tap_index + 1) * width],
            preferred_element_type=jnp.float32,
        )
    gate_value = jax.nn.sigmoid(preact)
    hidden = (preact * gate_value).astype(jnp.bfloat16)
    slope_term = gate_value * (1.0 + preact * (1.0 - gate_value))
    logits = (
        jnp.einsum("kc,nc->kn", head_weight, hidden, preferred_element_type=jnp.float32)
        + head_bias[:, None]
    )
    positions = jnp.arange(sample_count, dtype=jnp.float32)
    arrival = jnp.transpose(pick_index, (2, 0, 1)).astype(jnp.float32)[..., None]
    target = jnp.exp(-((positions - arrival) ** 2) / (2.0 * SIGMA * SIGMA)).reshape(2, cells)
    usable = jnp.broadcast_to(
        good_channel.astype(jnp.float32)[:, :, None], (patch_count, row_count, sample_count)
    ).reshape(1, cells)
    dlogit = (usable * (jax.nn.sigmoid(logits) - target)).astype(jnp.bfloat16)
    grad_head_weight = jnp.dot(dlogit, hidden, preferred_element_type=jnp.float32)
    grad_head_bias = jnp.sum(dlogit.astype(jnp.float32), axis=1)
    dact = jnp.einsum("kn,kc->nc", dlogit, head_weight, preferred_element_type=jnp.float32)
    dpre = (dact * slope_term).astype(jnp.bfloat16)
    grad_conv_bias = jnp.sum(dpre.astype(jnp.float32), axis=0)[None, :]
    blocks = [
        jnp.einsum("nc,nd->cd", window, dpre, preferred_element_type=jnp.float32)
        for window in shifted
    ]
    grad_conv_weight = jnp.concatenate(blocks, axis=0)
    dpad = jnp.pad(
        dpre.reshape(patch_count, row_count, sample_count, width), ((0, 0), (1, 1), (1, 1), (0, 0))
    )
    back = jnp.zeros((cells, width), jnp.float32)
    for tap_index in range(9):
        offset_row = tap_index // 3
        offset_col = tap_index % 3
        window = dpad[
            :,
            2 - offset_row : 2 - offset_row + row_count,
            2 - offset_col : 2 - offset_col + sample_count,
            :,
        ].reshape(cells, width)
        back = back + jnp.einsum(
            "nd,cd->nc",
            window,
            conv_weight[tap_index * width : (tap_index + 1) * width],
            preferred_element_type=jnp.float32,
        )
    grad_features = back.astype(jnp.bfloat16).reshape(patch_count, row_count, sample_count, width)
    return (grad_conv_weight, grad_conv_bias, grad_head_weight, grad_head_bias, grad_features)


def on_device(features, pick_index, good_channel, conv_weight, conv_bias, head_weight, head_bias):
    full_conv, full_bias, full_head = (
        lax.all_gather(conv_weight, "fsdp", axis=1, tiled=True),
        lax.all_gather(conv_bias, "fsdp", axis=1, tiled=True),
        lax.all_gather(head_weight, "fsdp", axis=1, tiled=True),
    )
    grad_kernel, grad_bias, grad_head, grad_hbias, grad_features = local_grads(
        features, pick_index, good_channel, full_conv, full_bias, full_head, head_bias
    )
    owned = lax.psum_scatter(grad_kernel, "dp", scatter_dimension=0, tiled=True)
    owned = lax.psum_scatter(owned, "fsdp", scatter_dimension=1, tiled=True)
    summed = lax.psum((grad_bias, grad_head, grad_hbias), "dp")
    bias_part, head_part = (
        lax.psum_scatter(summed[0], "fsdp", scatter_dimension=1, tiled=True),
        lax.psum_scatter(summed[1], "fsdp", scatter_dimension=1, tiled=True),
    )
    hbias_total = lax.psum(summed[2], "fsdp")
    return (owned, bias_part, head_part, hbias_total, grad_features)


def solution(mesh):
    return jax.shard_map(
        on_device,
        mesh=mesh,
        in_specs=(
            P(("dp", "fsdp"), None, None, None),
            P(("dp", "fsdp"), None, None),
            P(("dp", "fsdp"), None),
            P(None, "fsdp"),
            P(None, "fsdp"),
            P(None, "fsdp"),
            P(),
        ),
        out_specs=(
            P("dp", "fsdp"),
            P(None, "fsdp"),
            P(None, "fsdp"),
            P(),
            P(("dp", "fsdp"), None, None, None),
        ),
        check_vma=False,
    )
```

profile of v0, /device:TPU:0, one launch (start us, length us, event | category | flops | bytes accessed | tf_op | source)
XLA Modules:
  0.0 184.8 jit_solution(14172446390495054646)
XLA Ops:
  7.3 0.7 convert_bitcast_fusion.1
  7.9 0.6 dynamic-slice
  9.2 0.9 dynamic-update-slice
  10.0 8.3 %all-reduce.2 = bf16[128]{0:T(256)(128)(2,1)S(1)} all-reduce(bf16[128]{0:T(256)(128)(2,1)S(1)} %dynamic-update-slice), channel_id=1, replica_groups=mesh['dp'=8,'fsdp'=4] {'fsdp'}, use_global_device_ids=true, to_apply=%add.2 | all-reduce | flops 128 | bytes 512
  18.3 0.7 convert_bitcast_fusion
  19.0 5.2 %all-gather = bf16[4,32,2]{1,2,0:T(2,128)(2,1)S(1)} all-gather(bf16[1,32,2]{1,2,0:T(2,128)(2,1)} %bitcast.139), channel_id=1, replica_groups=mesh['dp'=8,'fsdp'=4] {'fsdp'}, dimensions={0}, use_global_device_ids=true | all-gather | bytes 640 | tf_op jit(solution)/shard_map/all_gather | solution.py:78
  24.5 6.0 %all_gather.10 = bf16[1152,128]{0,1:T(8,128)(2,1)S(1)} all-gather(bf16[1152,32]{0,1:T(8,128)(2,1)S(1)} %copy-done.2), channel_id=1, replica_groups=mesh['dp'=8,'fsdp'=4] {'fsdp'}, dimensions={1}, use_global_device_ids=true | all-gather | bytes 368640 | tf_op jit(solution)/shard_map/all_gather | solution.py:76
  30.5 3.5 %pad_slice_fusion.8 = (bf16[1,8,256,128]{3,2,1,0:T(8,128)(2,1)S(1)}, bf16[1,8,256,128]{3,2,1,0:T(8,128)(2,1)S(1)}, bf16[1,8,256,128]{3,2,1,0:T(8,128)(2,1)S(1)},...) fusion(bf16[1,8,256,128]{3,2,1,0:T(8,128)(2,1)} %param.7), kind=kLoop, calls=%fused_computation.51 | loop fusion | bytes 4718592 | tf_op jit(solution)/shard_map/slice | solution.py:18
  35.2 0.7 copy-done
  37.1 0.5 multiply_convert_fusion
  37.6 0.6 copy-done.3
  38.2 0.4 convert_reduce_fusion.1
  38.6 0.6 convert_reduce_fusion
  39.2 0.3 convolution_dynamic-update-slice_fusion.7
  39.9 0.3 convolution_dynamic-update-slice_fusion.5
  40.2 0.3 convolution_dynamic-update-slice_fusion.4
  40.6 0.3 fusion.10
  40.9 0.3 convolution_dynamic-update-slice_fusion.3
  41.9 0.3 convolution_dynamic-update-slice_fusion
  42.3 0.8 copy-done.1
  43.2 0.7 copy.19
  44.0 1.0 convolution_bitcast_fusion.1
  45.0 0.8 pad_slice_fusion
  48.1 58.1 %reduce-scatter.11.cloned.1.call-done = f32[144,128]{1,0:T(8,128)} async-done(((f32[1152,128]{1,0:T(8,128)}), f32[144,128]{1,0:T(8,128)}) %reduce-scatter.11.cloned.1.call-update) | async-done | bytes 73744 | tf_op jit(solution)/shard_map/reduce_scatter | solution.py:83
  106.2 1.6 copy.17
  107.9 1.1 fusion.1
  108.9 18.3 %reduce-scatter.15.cloned.1.call-done = f32[32,1]{1,0:T(8,128)} async-done(((f32[128,1]{1,0:T(8,128)}), f32[32,1]{1,0:T(8,128)}) %reduce-scatter.15.cloned.1.call-update) | async-done | bytes 144
  127.2 0.8 copy.20
  128.0 21.1 %reduce-scatter.17.cloned.1.call-done = f32[32,2]{1,0:T(8,128)} async-done(((f32[128,2]{1,0:T(8,128)}), f32[32,2]{1,0:T(8,128)}) %reduce-scatter.17.cloned.1.call-update) | async-done | bytes 272
  149.1 0.8 copy.22
  149.9 21.9 %all-reduce.3 = (f32[1,32]{1,0:T(1,128)}, f32[2,32]{1,0:T(2,128)}, f32[2]{0:T(128)S(1)}) all-reduce(f32[1,32]{1,0:T(1,128)S(1)} %copy.20, f32[2,32]{1,0:T(2,128)S(1)} %copy.22, f32[2]{0:T(128)S(1)} %get-tuple-element.43), channel_id=1, replica_groups=mesh['dp'=8,'fsdp'=4] {'dp'}, use_global_device_ids=true, to_apply=%region_3.4 | all-reduce | flops 98 | bytes 784 | tf_op jit(solution)/shard_map/psum | solution.py:85
  171.8 6.4 %psum.31 = f32[2]{0:T(128)} all-reduce(f32[2]{0:T(128)S(1)} %get-tuple-element.22), channel_id=1, replica_groups=mesh['dp'=8,'fsdp'=4] {'fsdp'}, use_global_device_ids=true, to_apply=%region_9.10 | all-reduce | flops 2 | bytes 16 | tf_op jit(solution)/shard_map/psum | solution.py:90
  (45 shorter events, 6.1 us)
Async XLA Ops:
  7.2 0.8 copy-start.4
  7.2 17.3 %copy-start.2 = (bf16[1152,32]{0,1:T(8,128)(2,1)S(1)}, bf16[1152,32]{0,1:T(8,128)(2,1)}, u32[]{:S(2)}) copy-start(bf16[1152,32]{0,1:T(8,128)(2,1)} %param.10) | copy-start | bytes 221188
  7.2 99.0 %reduce-scatter.11.cloned.1.call-start = ((), (), s32[]{:S(2)}) async-start(), calls=%async_computation.4 | async-start | bytes 663552 | tf_op jit(solution)/shard_map/reduce_scatter | solution.py:83
  34.8 1.0 copy-start
  37.6 0.7 copy-start.3
  42.3 0.8 copy-start.1
  43.1 84.1 %reduce-scatter.15.cloned.1.call-start = ((), (), s32[]{:S(2)}) async-start(), calls=%async_computation.6 | async-start | bytes 81920
  43.9 105.2 %reduce-scatter.17.cloned.1.call-start = ((), (), s32[]{:S(2)}) async-start(), calls=%async_computation.7 | async-start | bytes 81920
  45.0 133.3 %reduce-scatter.13.cloned.1.call-start = ((), (), s32[]{:S(2)}) async-start(), calls=%async_computation.5 | async-start | bytes 163840
Sparse Core Ops, SparseCore 0:
  43.2 62.9 reduce-scatter.10
  108.8 18.4 reduce-scatter.14
  129.7 19.3 reduce-scatter.16
  152.1 19.5 reduce-scatter.12
where the time goes:
time: 185 us
  waiting for transfers between devices  97.5 us (53%)
  blocking collectives  47.8 us (26%)
  between operations  14.7 us (8%)
  local copies, waits for them, and re-layouts  12.1 us (7%)
  matrix products  11.1 us (6%)
    reduce_scatter x1, waiting for transfers between devices, on_device(): owned = lax.psum_scatter(grad_kernel, 'dp', scatter_dimension=0, tiled=True)  58.1 us
    unnamed x7, waiting for transfers between devices  39.4 us
    psum x1, blocking collectives, on_device(): summed = lax.psum((grad_bias, grad_head, grad_hbias), 'dp')  21.9 us
    unnamed x1, blocking collectives  8.31 us
    unnamed x24, local copies, waits for them, and re-layouts  7.84 us
    psum x1, blocking collectives, on_device(): hbias_total = lax.psum(summed[2], 'fsdp')  6.4 us
    all_gather x1, blocking collectives, on_device(): lax.all_gather(conv_weight, 'fsdp', axis=1, tiled=True)  6 us
    all_gather x1, blocking collectives, on_device(): lax.all_gather(head_weight, 'fsdp', axis=1, tiled=True)  5.16 us
  transfers between devices with their start and end apart: 4, of which 3 were waited for; matrix products, arithmetic and copies ran while one was open for 5% of the time, Pallas kernels for 0%

commit v1 on v0

--- a/solution.py
+++ b/solution.py
@@ -1,9 +1,32 @@
+import functools
 import jax
 import jax.numpy as jnp
 from jax import lax
 from jax.sharding import PartitionSpec as P
 
 SIGMA = 20
+
+
+def apply_words_on(array_in, group_axis):
+    n_shards = lax.axis_size(group_axis)
+    e_next = range(n_shards)
+    queue = list(map(lambda i: (i, (i + 1) % n_shards), e_next))
+    v_now = range(n_shards)
+    x_now = map(lambda i: (i, (i - 1) % n_shards), v_now)
+    so_far_all = list(x_now)
+    plain, right_arr = ([array_in], [array_in])
+    for _ in range(n_shards // 2):
+        plain.append(lax.ppermute(plain[-1], group_axis, queue))
+    u = 0
+    while u < (n_shards - 1) // 2:
+        right_arr.append(lax.ppermute(right_arr[-1], group_axis, so_far_all))
+        u = u + 1
+    y2 = jnp.concatenate([*plain[::-1], *right_arr[1:]], axis=1)
+    current_value = lax.axis_index(group_axis)
+    return jnp.roll(y2, (current_value - n_shards // 2) * array_in.shape[1], axis=1)
+
+
+serve_goods = functools.partial(apply_words_on, group_axis="fsdp")
 
 
 def local_grads(features, pick_index, good_channel, conv_weight, conv_bias, head_weight, head_bias):
@@ -73,7 +96,7 @@
 
 def on_device(features, pick_index, good_channel, conv_weight, conv_bias, head_weight, head_bias):
     full_conv, full_bias, full_head = (
-        lax.all_gather(conv_weight, "fsdp", axis=1, tiled=True),
+        serve_goods(conv_weight),
         lax.all_gather(conv_bias, "fsdp", axis=1, tiled=True),
         lax.all_gather(head_weight, "fsdp", axis=1, tiled=True),
     )

time: 185 us -> 192 us (1.038)
  matrix products: 11.1 us -> 31.8 us
  waiting for transfers between devices: 97.5 us -> 83.2 us
  blocking collectives: 47.8 us -> 40 us
  local copies, waits for them, and re-layouts: 12.1 us -> 18 us
  starting transfers between devices: 0.16 us -> 2.72 us
    dot_general x9, matrix products: 3.32 us -> 18.1 us  [local_grads(): jnp.einsum('nd,cd->nc', window, conv_weight[tap_index * width:(tap_index...]
    reduce_scatter x1, waiting for transfers between devices: 58.1 us -> 46.7 us  [on_device(): owned = lax.psum_scatter(grad_kernel, 'dp', scatter_dimension=0, tiled=True)]
    all_gather x1 -> x0, blocking collectives: 6 us -> none  [on_device(): lax.all_gather(conv_weight, 'fsdp', axis=1, tiled=True)]
    dot_general x9, matrix products: 3.06 us -> 8.73 us  [local_grads(): jnp.einsum('nc,nd->cd', window, dpre, preferred_element_type=jnp.float32)]
    unnamed x24 -> x57, local copies, waits for them, and re-layouts: 7.84 us -> 11.4 us
    unnamed x7, waiting for transfers between devices: 39.4 us -> 36.5 us
    ppermute x0 -> x3, starting transfers between devices: none -> 2.55 us  [the longest x1 1.99 us: apply_words_on(): right_arr.append(lax.ppermute(right_arr[-1], group_axis, so_far_all))]
    unnamed x1, blocking collectives: 8.31 us -> 6.3 us
  transfers between devices with their start and end apart: 4 -> 7, of which waited for: 3 -> 3; matrix products, arithmetic and copies ran while one was open for 5% -> 16% of each run, Pallas kernels for 0% -> 0%
where the time goes in v1:
time: 192 us; the launch traced here: 191 us
  waiting for transfers between devices  83.2 us (43%)
  blocking collectives  40 us (21%)
  matrix products  31.8 us (17%)
  local copies, waits for them, and re-layouts  18 us (9%)
  between operations  14.7 us (8%)
  starting transfers between devices  2.72 us (1%)
    reduce_scatter x1, waiting for transfers between devices, on_device(): owned = lax.psum_scatter(grad_kernel, 'dp', scatter_dimension=0, tiled=True)  46.7 us
    unnamed x7, waiting for transfers between devices  36.5 us
    psum x1, blocking collectives, on_device(): summed = lax.psum((grad_bias, grad_head, grad_hbias), 'dp')  21.9 us
    dot_general x9, matrix products, local_grads(): jnp.einsum('nd,cd->nc', window, conv_weight[tap_index * width:(tap_index...  18.1 us
    unnamed x57, local copies, waits for them, and re-layouts  11.4 us
    dot_general x9, matrix products, local_grads(): jnp.einsum('nc,nd->cd', window, dpre, preferred_element_type=jnp.float32)  8.73 us
    psum x1, blocking collectives, on_device(): hbias_total = lax.psum(summed[2], 'fsdp')  6.4 us
    unnamed x1, blocking collectives  6.3 us
  transfers between devices with their start and end apart: 7, of which 3 were waited for; matrix products, arithmetic and copies ran while one was open for 16% of the time, Pallas kernels for 0%

profile of v1, /device:TPU:0, one launch (start us, length us, event | category | flops | bytes accessed | tf_op | source)
XLA Modules:
  0.0 191.2 jit_solution(10389282130890610651)
XLA Ops:
  7.7 2.0 %collective-permute-start.2 = (bf16[1152,32]{0,1:T(8,128)(2,1)}, bf16[1152,32]{0,1:T(8,128)(2,1)S(1)}, u32[]{:S(2)}, u32[]{:S(2)}) collective-permute-start(bf16[1152,32]{0,1:T(8,128)(2,1)} %param.10), channel_id=1, source_target_pairs={{0,3},{1,0},{2,1},{3,2},{4,7},{5,4},{6,5},{7,6},{8,11},{9,8},{10,9... | collective-permute-start | bytes 221192 | tf_op jit(solution)/shard_map/ppermute | solution.py:22
  11.1 4.5 %pad_slice_fusion.14 = (bf16[1,8,256,128]{3,2,1,0:T(8,128)(2,1)}, bf16[1,8,256,128]{3,2,1,0:T(8,128)(2,1)S(1)}, bf16[1,8,256,128]{3,2,1,0:T(8,128)(2,1)S(1)}, bf...) fusion(bf16[1,8,256,128]{3,2,1,0:T(8,128)(2,1)} %param.7), kind=kLoop, calls=%fused_computation.58 | loop fusion | bytes 4718592 | tf_op jit(solution)/shard_map/slice | solution.py:41
  18.4 6.3 %all-reduce.2 = bf16[128]{0:T(256)(128)(2,1)S(1)} all-reduce(bf16[128]{0:T(256)(128)(2,1)S(1)} %dynamic-update-slice), channel_id=1, replica_groups=mesh['dp'=8,'fsdp'=4] {'fsdp'}, use_global_device_ids=true, to_apply=%add.2 | all-reduce | flops 128 | bytes 512
  25.5 5.4 %all-gather = bf16[4,32,2]{1,2,0:T(2,128)(2,1)S(1)} all-gather(bf16[1,32,2]{1,2,0:T(2,128)(2,1)S(1)} %bitcast.141), channel_id=1, replica_groups=mesh['dp'=8,'fsdp'=4] {'fsdp'}, dimensions={0}, use_global_device_ids=true | all-gather | bytes 640 | tf_op jit(solution)/shard_map/all_gather | solution.py:101
  31.1 0.9 copy-done.12
  39.1 1.0 convolution_dynamic-update-slice_fusion.7
  40.1 1.3 fusion.44
  41.3 1.0 convolution_dynamic-update-slice_fusion.6
  42.4 1.0 convolution_dynamic-update-slice_fusion.5
  43.3 1.0 convolution_dynamic-update-slice_fusion.4
  44.3 1.0 fusion.25
  45.3 1.0 convolution_dynamic-update-slice_fusion.3
  46.3 1.0 convolution_dynamic-update-slice_fusion.2
  47.2 1.0 convolution_dynamic-update-slice_fusion.1
  48.2 1.0 convolution_dynamic-update-slice_fusion
  49.2 2.0 %pad_slice_fusion.7 = (bf16[1,8,256,128]{3,2,1,0:T(8,128)(2,1)}, bf16[1,8,256,128]{3,2,1,0:T(8,128)(2,1)}, bf16[1,8,256,128]{3,2,1,0:T(8,128)(2,1)S(1)}, bf16[1,...) fusion(bf16[1,8,256,128]{3,2,1,0:T(8,128)(2,1)S(1)} %bitcast.105), kind=kLoop, calls=%fused_computation.51 | loop fusion | bytes 4718592 | tf_op jit(solution)/shard_map/slice | solution.py:81
  51.3 1.0 fusion.28
  52.3 1.1 fusion.32
  54.1 2.1 %fusion.36 = f32[2048,128]{1,0:T(8,128)} fusion(bf16[2048,128]{1,0:T(8,128)(2,1)S(1)} %bitcast.129, bf16[1152,256]{0,1:T(8,128)(2,1)} %copy-done.11, s32[]{:T(128)S(6)} %add.150, s32[]{:T(128)S(6)} %select_n.14), kind=kOutput, calls=%fused_computation.78 | convolution fusion | flops 67108864 | bytes 1605640 | tf_op jit(solution)/shard_map/nd,cd->nc/dot_general | solution.py:87
  56.2 2.1 %fusion.40 = f32[2048,128]{1,0:T(8,128)} fusion(bf16[2048,128]{1,0:T(8,128)(2,1)S(1)} %bitcast.128, bf16[1152,256]{0,1:T(8,128)(2,1)} %copy-done.11, s32[]{:T(128)S(6)} %add.149, s32[]{:T(128)S(6)} %select_n.14), kind=kOutput, calls=%fused_computation.82 | convolution fusion | flops 67108864 | bytes 1605640 | tf_op jit(solution)/shard_map/nd,cd->nc/dot_general | solution.py:87
  58.3 2.0 %fusion.47 = f32[2048,128]{1,0:T(8,128)} fusion(bf16[2048,128]{1,0:T(8,128)(2,1)S(1)} %bitcast.127, bf16[1152,256]{0,1:T(8,128)(2,1)} %copy-done.11, s32[]{:T(128)S(6)} %add.147, s32[]{:T(128)S(6)} %select_n.14), kind=kOutput, calls=%fused_computation.89 | convolution fusion | flops 67108864 | bytes 1605640 | tf_op jit(solution)/shard_map/nd,cd->nc/dot_general | solution.py:87
  60.4 2.1 %fusion.51 = f32[2048,128]{1,0:T(8,128)} fusion(bf16[2048,128]{1,0:T(8,128)(2,1)S(1)} %bitcast.126, bf16[1152,256]{0,1:T(8,128)(2,1)} %copy-done.11, s32[]{:T(128)S(6)} %add.146, s32[]{:T(128)S(6)} %select_n.14), kind=kOutput, calls=%fused_computation.93 | convolution fusion | flops 67108864 | bytes 1605640 | tf_op jit(solution)/shard_map/nd,cd->nc/dot_general | solution.py:87
  62.5 1.0 convolution_bitcast_fusion.2
  63.5 2.4 %fusion.55 = f32[2048,128]{1,0:T(8,128)} fusion(bf16[2048,128]{1,0:T(8,128)(2,1)} %bitcast.125, bf16[1152,256]{0,1:T(8,128)(2,1)} %copy-done.11, s32[]{:T(128)S(6)} %add.145, s32[]{:T(128)S(6)} %select_n.14), kind=kOutput, calls=%fused_computation.97 | convolution fusion | flops 67108864 | bytes 1605640 | tf_op jit(solution)/shard_map/nd,cd->nc/dot_general | solution.py:87
  65.9 46.7 %reduce-scatter.11.cloned.1.call-done = f32[144,128]{1,0:T(8,128)} async-done(((f32[1152,128]{1,0:T(8,128)}), f32[144,128]{1,0:T(8,128)}) %reduce-scatter.11.cloned.1.call-update) | async-done | bytes 73744 | tf_op jit(solution)/shard_map/reduce_scatter | solution.py:106
  112.7 1.6 copy.21
  114.3 4.0 %fusion.15 = bf16[2048,128]{1,0:T(8,128)(2,1)} fusion(f32[2048,128]{1,0:T(8,128)S(1)} %fusion.28, f32[2048,128]{1,0:T(8,128)S(1)} %fusion.32, f32[2048,128]{1,0:T(8,128)} %fusion.36, f32[2048,128]{1,0:T(8,128)} %fusion.40, f32[2048,128]{1,0:T(8,128)S(1)} %copy-done.5, f32[2048,128]{1,0:T(8,128)} %fusion.47, f32[2048,128]{1,0:T(8,128)} %fusion.51, ...), kind=kOutput, calls=%fused_computation.19 | convolution fusion | flops 69468160 | bytes 9469956 | tf_op jit(solution)/shard_map/nd,cd->nc/dot_general | solution.py:87
  118.3 15.3 %reduce-scatter.15.cloned.1.call-done = f32[32,1]{1,0:T(8,128)} async-done(((f32[128,1]{1,0:T(8,128)}), f32[32,1]{1,0:T(8,128)}) %reduce-scatter.15.cloned.1.call-update) | async-done | bytes 144
  133.7 0.8 copy.24
  134.5 21.1 %reduce-scatter.17.cloned.1.call-done = f32[32,2]{1,0:T(8,128)} async-done(((f32[128,2]{1,0:T(8,128)}), f32[32,2]{1,0:T(8,128)}) %reduce-scatter.17.cloned.1.call-update) | async-done | bytes 272
  156.4 21.9 %all-reduce.3 = (f32[1,32]{1,0:T(1,128)}, f32[2,32]{1,0:T(2,128)}, f32[2]{0:T(128)S(1)}) all-reduce(f32[1,32]{1,0:T(1,128)S(1)} %copy.24, f32[2,32]{1,0:T(2,128)S(1)} %copy.26, f32[2]{0:T(128)S(1)} %get-tuple-element.43), channel_id=1, replica_groups=mesh['dp'=8,'fsdp'=4] {'dp'}, use_global_device_ids=true, to_apply=%region_3.4 | all-reduce | flops 98 | bytes 784 | tf_op jit(solution)/shard_map/psum | solution.py:108
  178.3 6.4 %psum.31 = f32[2]{0:T(128)} all-reduce(f32[2]{0:T(128)S(1)} %get-tuple-element.22), channel_id=1, replica_groups=mesh['dp'=8,'fsdp'=4] {'fsdp'}, use_global_device_ids=true, to_apply=%region_9.10 | all-reduce | flops 2 | bytes 16 | tf_op jit(solution)/shard_map/psum | solution.py:113
  (84 shorter events, 13.8 us)
Async XLA Ops:
  7.2 105.5 %reduce-scatter.11.cloned.1.call-start = ((), (), s32[]{:S(2)}) async-start(), calls=%async_computation.4 | async-start | bytes 663552 | tf_op jit(solution)/shard_map/reduce_scatter | solution.py:106
  7.2 17.5 %collective-permute-start = (bf16[1152,32]{0,1:T(8,128)(2,1)}, bf16[1152,32]{0,1:T(8,128)(2,1)S(1)}, u32[]{:S(2)}, u32[]{:S(2)}) collective-permute-start(bf16[1152,32]{0,1:T(8,128)(2,1)} %param.10), channel_id=1, source_target_pairs={{0,1},{1,2},{2,3},{3,0},{4,5},{5,6},{6,7},{7,4},{8,9},{9,10},{10,1... | collective-permute-start | bytes 221192 | tf_op jit(solution)/shard_map/ppermute | solution.py:19
  7.7 24.2 %collective-permute-start.2 = (bf16[1152,32]{0,1:T(8,128)(2,1)}, bf16[1152,32]{0,1:T(8,128)(2,1)S(1)}, u32[]{:S(2)}, u32[]{:S(2)}) collective-permute-start(bf16[1152,32]{0,1:T(8,128)(2,1)} %param.10), channel_id=1, source_target_pairs={{0,3},{1,0},{2,1},{3,2},{4,7},{5,4},{6,5},{7,6},{8,11},{9,8},{10,9... | collective-permute-start | bytes 221192 | tf_op jit(solution)/shard_map/ppermute | solution.py:22
  10.4 0.7 copy-start.14
  15.6 19.0 %copy-start.1 = (bf16[1,8,256,128]{3,2,1,0:T(8,128)(2,1)}, bf16[1,8,256,128]{3,2,1,0:T(8,128)(2,1)S(1)}, u32[]{:S(2)}) copy-start(bf16[1,8,256,128]{3,2,1,0:T(8,128)(2,1)S(1)} %get-tuple-element.32) | copy-start | bytes 1572868
  15.7 0.7 copy-start.17
  17.5 0.7 copy-start.15
  24.7 6.3 %collective-permute-start.1 = (bf16[1152,32]{0,1:T(8,128)(2,1)S(1)}, bf16[1152,32]{0,1:T(8,128)(2,1)S(1)}, u32[]{:S(2)}, u32[]{:S(2)}) collective-permute-start(bf16[1152,32]{0,1:T(8,128)(2,1)S(1)} %collective-permute-done), channel_id=1, source_target_pairs={{0,1},{1,2},{2,3},{3,0},{4,5},{5,6},{6,7},{7,4},{8,9},{9,10},{10,1... | collective-permute-start | bytes 221192 | tf_op jit(solution)/shard_map/ppermute | solution.py:19
  24.8 0.7 copy-start.13
  31.0 0.9 copy-start.12
  32.0 8.1 %copy-start.11 = (bf16[1152,256]{0,1:T(8,128)(2,1)}, bf16[1152,256]{0,1:T(8,128)(2,1)S(1)}, u32[]{:S(2)}) copy-start(bf16[1152,256]{0,1:T(8,128)(2,1)S(1)} %constant_dynamic-update-slice_fusion) | copy-start | bytes 1769476
  33.0 1.0 copy-start
  34.6 1.0 copy-start.3
  35.7 1.0 copy-start.4
  37.4 1.7 copy-start.9
  37.4 0.7 copy-start.16
  41.3 1.0 copy-start.2
  49.2 84.5 %reduce-scatter.15.cloned.1.call-start = ((), (), s32[]{:S(2)}) async-start(), calls=%async_computation.6 | async-start | bytes 81920
  52.3 1.8 copy-start.8
  54.1 2.1 %copy-start.7 = (bf16[1,8,256,128]{3,2,1,0:T(8,128)(2,1)S(1)}, bf16[1,8,256,128]{3,2,1,0:T(8,128)(2,1)}, u32[]{:S(2)}) copy-start(bf16[1,8,256,128]{3,2,1,0:T(8,128)(2,1)} %get-tuple-element.27) | copy-start | bytes 1572868
  56.2 2.1 %copy-start.6 = (bf16[1,8,256,128]{3,2,1,0:T(8,128)(2,1)S(1)}, bf16[1,8,256,128]{3,2,1,0:T(8,128)(2,1)}, u32[]{:S(2)}) copy-start(bf16[1,8,256,128]{3,2,1,0:T(8,128)(2,1)} %get-tuple-element.26) | copy-start | bytes 1572868
  60.4 2.1 %copy-start.10 = (bf16[2048,128]{1,0:T(8,128)(2,1)S(1)}, bf16[2048,128]{1,0:T(8,128)(2,1)}, u32[]{:S(2)}) copy-start(bf16[2048,128]{1,0:T(8,128)(2,1)} %copy-done.9) | copy-start | bytes 1572868
  62.4 93.1 %reduce-scatter.17.cloned.1.call-start = ((), (), s32[]{:S(2)}) async-start(), calls=%async_computation.7 | async-start | bytes 81920
  63.5 50.9 %copy-start.5 = (f32[2048,128]{1,0:T(8,128)S(1)}, f32[2048,128]{1,0:T(8,128)}, u32[]{:S(2)}) copy-start(f32[2048,128]{1,0:T(8,128)} %fusion.44) | copy-start | bytes 3145732
  63.5 121.2 %reduce-scatter.13.cloned.1.call-start = ((), (), s32[]{:S(2)}) async-start(), calls=%async_computation.5 | async-start | bytes 163840
Sparse Core Ops, SparseCore 0:
  49.3 63.2 reduce-scatter.10
  115.2 18.4 reduce-scatter.14
  136.1 19.4 reduce-scatter.16
  158.6 19.5 reduce-scatter.12
